TPU v7x, 32 devices: a whole 2x2x4 slice. The times are simulated.
32 devices in a mesh: pipe: 8 (over y, x, core), dp: 4 (over z).
Axes of the slice: x: 2, y: 2, z: 4, core: 2. Of those that a mesh axis runs over, the one named last changes fastest.
Arguments:
- inputs: bfloat16 [4, 128, 6144], P(None, 'dp'), may hold values from -6 to 6
- cotangent: bfloat16 [4, 128, 6144], P(None, 'dp'), may hold values from -6 to 6
- gains: float32 [8, 6144], P('pipe'), may hold values from 0.5 to 1.5
- w_value: bfloat16 [8, 6144, 128], P('pipe'), may hold values from -0.078125 to 0.078125
- w_out: bfloat16 [8, 128, 6144], P('pipe'), may hold values from -0.5 to 0.5
Outputs:
- grad_value: float32 [8, 6144, 128], P('pipe')
- grad_out: float32 [8, 128, 6144], P('pipe')
- grad_gain: float32 [8, 6144], P('pipe')
All inputs are finite; a program needn't handle non-finite values.
Results may differ from a plain program's by a relative error of at most 0.02.
Values may be sent and summed in bfloat16 or wider, within the bound.
A program may use at most 64 MiB of HBM per device.

v0:
```python
import jax
import jax.numpy as jnp
from jax import lax
from jax.sharding import PartitionSpec as P

epsilon = 1e-05


def shortened(x):
    return jax.tree.map(lambda a: a.astype(jnp.bfloat16) if a.dtype == jnp.float32 else a, x)


def with_halo(cells, sides, width):
    for axis, dim in sides:
        count = lax.axis_size(axis)
        ends = count - 1
        head = lax.slice_in_dim(cells, 0, width, axis=dim)
        tail = lax.slice_in_dim(cells, cells.shape[dim] - width, cells.shape[dim], axis=dim)
        cells = jnp.concatenate(
            [
                lax.ppermute(tail, axis, [(i, (i + 1) % count) for i in range(ends)]),
                cells,
                lax.ppermute(head, axis, [((i + 1) % count, i) for i in range(ends)]),
            ],
            axis=dim,
        )
    return cells


def normalize(floats):
    inv_rms = lax.rsqrt(jnp.mean(floats * floats, axis=-1, keepdims=True) + epsilon)
    return (floats * inv_rms, inv_rms)


def section_forward(hidden, gain_row, value_weight, out_weight):
    floats = hidden.astype(jnp.float32)
    normed, inv_rms = normalize(floats)
    mixed_rows = (normed * gain_row).astype(jnp.bfloat16)
    values = jnp.dot(mixed_rows, value_weight, preferred_element_type=jnp.float32).astype(
        jnp.bfloat16
    )
    branch = jnp.dot(values, out_weight, preferred_element_type=jnp.float32)
    return (floats + branch).astype(jnp.bfloat16)


def per_device(inputs, cotangent, gains, w_value, w_out):
    sections = lax.axis_size("pipe")
    position = lax.axis_index("pipe")
    batches = inputs.shape[0]
    gain_row = gains[0]
    value_weight = w_value[0]
    out_weight = w_out[0]

    def spare_turn(operand):
        stashed, arrived, sum_value, sum_out, sum_gain, chosen = operand
        return (jnp.zeros_like(arrived), stashed, sum_value, sum_out, sum_gain)

    def forward_turn(operand):
        stashed, arrived, sum_value, sum_out, sum_gain, chosen = operand
        fresh = lax.dynamic_index_in_dim(inputs, chosen, 0, keepdims=False)
        hidden = jnp.where(position == 0, fresh, arrived)
        stashed = lax.dynamic_update_index_in_dim(stashed, hidden, chosen, 0)
        result = section_forward(hidden, gain_row, value_weight, out_weight)
        return (result, stashed, sum_value, sum_out, sum_gain)

    def backward_turn(operand):
        stashed, arrived, sum_value, sum_out, sum_gain, chosen = operand
        hidden = lax.dynamic_index_in_dim(stashed, chosen, 0, keepdims=False)
        top_grad = lax.dynamic_index_in_dim(cotangent, chosen, 0, keepdims=False)
        upstream = jnp.where(position == sections - 1, top_grad, arrived)
        floats = hidden.astype(jnp.float32)
        normed, inv_rms = normalize(floats)
        mixed_rows = (normed * gain_row).astype(jnp.bfloat16)
        values = jnp.dot(mixed_rows, value_weight, preferred_element_type=jnp.float32).astype(
            jnp.bfloat16
        )
        dvalues = jnp.einsum(
            "tj,kj->tk", upstream, out_weight, preferred_element_type=jnp.float32
        ).astype(jnp.bfloat16)
        dmixed = jnp.einsum("tk,dk->td", dvalues, value_weight, preferred_element_type=jnp.float32)
        sum_out = sum_out + jnp.einsum(
            "tk,tj->kj", values, upstream, preferred_element_type=jnp.float32
        )
        sum_value = sum_value + jnp.einsum(
            "td,tk->dk", mixed_rows, dvalues, preferred_element_type=jnp.float32
        )
        sum_gain = sum_gain + jnp.sum(dmixed * normed, axis=0)
        dnormed = dmixed * gain_row
        inner = jnp.mean(dnormed * normed, axis=-1, keepdims=True)
        upper = upstream.astype(jnp.float32)
        downstream = (upper + inv_rms * (dnormed - normed * inner)).astype(jnp.bfloat16)
        return (downstream, stashed, sum_value, sum_out, sum_gain)

    def work(tick, state):
        stashed, arrived, sum_value, sum_out, sum_gain = state
        offset = tick - position
        is_forward = offset % 2 == 0
        forward_index = offset // 2
        backward_index = (tick - 2 * sections + 1 + position) // 2
        batch_index = jnp.where(is_forward, forward_index, backward_index)
        active = (batch_index >= 0) & (batch_index < batches)
        chosen = jnp.clip(batch_index, 0, batches - 1)
        mode = jnp.where(active, jnp.where(is_forward, 1, 2), 0).astype(jnp.int32)
        return lax.switch(
            mode,
            [spare_turn, forward_turn, backward_turn],
            (stashed, arrived, sum_value, sum_out, sum_gain, chosen),
        )

    def pass_along(payload, tick):
        padded = with_halo(shortened(payload[None]), (("pipe", 0),), 1)
        forward_next = (tick + 1 - position) % 2 == 0
        return jnp.where(forward_next, padded[0], padded[2])

    def one_round(round_index, state):
        payload, stashed, sum_value, sum_out, sum_gain = work(2 * round_index, state)
        arrived = pass_along(payload, 2 * round_index)
        payload, stashed, sum_value, sum_out, sum_gain = work(
            2 * round_index + 1, (stashed, arrived, sum_value, sum_out, sum_gain)
        )
        arrived = pass_along(payload, 2 * round_index + 1)
        return (stashed, arrived, sum_value, sum_out, sum_gain)

    first_stop = sections // 4 + batches - 1
    second_stop = 3 * sections // 4
    last_stop = sections + batches - 1
    state = (
        jnp.zeros_like(inputs),
        jnp.zeros_like(inputs[0]),
        jnp.zeros(value_weight.shape, jnp.float32),
        jnp.zeros(out_weight.shape, jnp.float32),
        jnp.zeros(gain_row.shape, jnp.float32),
    )
    state = lax.fori_loop(0, first_stop, one_round, state)
    stashed, arrived, sum_value, sum_out, sum_gain = state
    state = lax.fori_loop(
        first_stop, second_stop, one_round, (stashed, arrived, sum_value, sum_out, sum_gain)
    )
    stashed, arrived, sum_value, sum_out, sum_gain = state
    state = lax.fori_loop(
        second_stop, last_stop, one_round, (stashed, arrived, sum_value, sum_out, sum_gain)
    )
    stashed, arrived, sum_value, sum_out, sum_gain = state
    low_parts = lax.optimization_barrier(
        (
            sum_value.astype(jnp.bfloat16),
            sum_out.astype(jnp.bfloat16),
            sum_gain.astype(jnp.bfloat16),
        )
    )
    total_value, total_out, total_gain = (
        lax.psum(low_parts[0].astype(jnp.float32).astype(jnp.bfloat16), "dp").astype(jnp.float32),
        lax.psum(low_parts[1].astype(jnp.float32).astype(jnp.bfloat16), "dp").astype(jnp.float32),
        lax.psum(low_parts[2].astype(jnp.float32).astype(jnp.bfloat16), "dp").astype(jnp.float32),
    )
    return (total_value[None], total_out[None], total_gain[None])


def solution(mesh):
    placed = (
        P(None, "dp", None),
        P(None, "dp", None),
        P("pipe", None),
        P("pipe", None, None),
        P("pipe", None, None),
    )
    return jax.shard_map(
        per_device,
        mesh=mesh,
        in_specs=placed,
        out_specs=(P("pipe", None, None), P("pipe", None, None), P("pipe", None)),
        check_vma=False,
    )
```

profile of v0, /device:TPU:0, one launch (start us, length us, event | category | flops | bytes accessed | tf_op | source)
XLA Modules:
  0.0 698.2 jit_solution(17372110360858090637)
XLA Ops:
  13.2 185.8 %while.61 = (s32[]{:T(128)}, bf16[4,32,6144]{2,1,0:T(8,128)(2,1)}, bf16[32,6144]{1,0:T(8,128)(2,1)}, f32[6144,128]{1,0:T(8,128)}, f32[128,6144]{1,0:T(8,128)}, /...) while((s32[]{:T(128)}, bf16[4,32,6144]{2,1,0:T(8,128)(2,1)}, ...), condition=%wide.region_15.16_spmd, body=%wide.region_0.15_spmd.sunk | while | flops 517882016 | bytes 62575520 | solution.py:134
  13.3 6.4 conditional.12
  28.3 12.6 %collective-permute-start.2 = (bf16[1,32,6144]{2,1,0:T(8,128)(2,1)}, bf16[1,32,6144]{2,1,0:T(8,128)(2,1)}, u32[]{:S(2)}, u32[]{:S(2)}) collective-permute-start(bf16[1,32,6144]{2,1,0:T(8,128)(2,1)} %get-tuple-element.1766), channel_id=1, source_target_pairs={{0,4},{4,8},{8,12},{12,16},{16,20},{20,24},{24,28},{1,5},{5,9},{9,... | collective-permute-start | bytes 1179656 | tf_op jit(solution)/shard_map/while/body/eval_jaxpr/ppermute | solution.py:21
  42.2 2.6 collective-permute-done.3
  46.6 6.4 conditional.12
  56.4 6.6 collective-permute-done.1
  65.6 14.3 %collective-permute-start.2 = (bf16[1,32,6144]{2,1,0:T(8,128)(2,1)}, bf16[1,32,6144]{2,1,0:T(8,128)(2,1)}, u32[]{:S(2)}, u32[]{:S(2)}) collective-permute-start(bf16[1,32,6144]{2,1,0:T(8,128)(2,1)} %get-tuple-element.1766), channel_id=1, source_target_pairs={{0,4},{4,8},{8,12},{12,16},{16,20},{20,24},{24,28},{1,5},{5,9},{9,... | collective-permute-start | bytes 1179656 | tf_op jit(solution)/shard_map/while/body/eval_jaxpr/ppermute | solution.py:21
  81.3 2.6 collective-permute-done.3
  85.7 6.4 conditional.12
  95.5 6.6 collective-permute-done.1
  104.7 14.3 %collective-permute-start.2 = (bf16[1,32,6144]{2,1,0:T(8,128)(2,1)}, bf16[1,32,6144]{2,1,0:T(8,128)(2,1)}, u32[]{:S(2)}, u32[]{:S(2)}) collective-permute-start(bf16[1,32,6144]{2,1,0:T(8,128)(2,1)} %get-tuple-element.1766), channel_id=1, source_target_pairs={{0,4},{4,8},{8,12},{12,16},{16,20},{20,24},{24,28},{1,5},{5,9},{9,... | collective-permute-start | bytes 1179656 | tf_op jit(solution)/shard_map/while/body/eval_jaxpr/ppermute | solution.py:21
  124.7 6.4 conditional.12
  134.6 6.6 collective-permute-done.1
  143.7 14.5 %collective-permute-start.2 = (bf16[1,32,6144]{2,1,0:T(8,128)(2,1)}, bf16[1,32,6144]{2,1,0:T(8,128)(2,1)}, u32[]{:S(2)}, u32[]{:S(2)}) collective-permute-start(bf16[1,32,6144]{2,1,0:T(8,128)(2,1)} %get-tuple-element.1766), channel_id=1, source_target_pairs={{0,4},{4,8},{8,12},{12,16},{16,20},{20,24},{24,28},{1,5},{5,9},{9,... | collective-permute-start | bytes 1179656 | tf_op jit(solution)/shard_map/while/body/eval_jaxpr/ppermute | solution.py:21
  164.8 8.3 %collective-permute-start = (bf16[1,32,6144]{2,1,0:T(8,128)(2,1)}, bf16[1,32,6144]{2,1,0:T(8,128)(2,1)}, u32[]{:S(2)}, u32[]{:S(2)}) collective-permute-start(bf16[1,32,6144]{2,1,0:T(8,128)(2,1)} %get-tuple-element.1764), channel_id=1, source_target_pairs={{0,4},{4,8},{8,12},{12,16},{16,20},{20,24},{24,28},{1,5},{5,9},{9,... | collective-permute-start | bytes 1179656 | tf_op jit(solution)/shard_map/while/body/eval_jaxpr/ppermute | solution.py:21
  174.4 6.9 collective-permute-done.1
  183.9 9.5 %collective-permute-start.2 = (bf16[1,32,6144]{2,1,0:T(8,128)(2,1)}, bf16[1,32,6144]{2,1,0:T(8,128)(2,1)}, u32[]{:S(2)}, u32[]{:S(2)}) collective-permute-start(bf16[1,32,6144]{2,1,0:T(8,128)(2,1)} %get-tuple-element.1766), channel_id=1, source_target_pairs={{0,4},{4,8},{8,12},{12,16},{16,20},{20,24},{24,28},{1,5},{5,9},{9,... | collective-permute-start | bytes 1179656 | tf_op jit(solution)/shard_map/while/body/eval_jaxpr/ppermute | solution.py:21
  199.8 14.3 %collective-permute-start.8 = (bf16[1,32,6144]{2,1,0:T(8,128)(2,1)}, bf16[1,32,6144]{2,1,0:T(8,128)(2,1)}, u32[]{:S(2)}, u32[]{:S(2)}) collective-permute-start(bf16[1,32,6144]{2,1,0:T(8,128)(2,1)} %get-tuple-element.1514), channel_id=1, source_target_pairs={{0,4},{4,8},{8,12},{12,16},{16,20},{20,24},{24,28},{1,5},{5,9},{9,... | collective-permute-start | bytes 1179656 | tf_op jit(solution)/shard_map/while/body/eval_jaxpr/ppermute | solution.py:21
  220.6 8.8 %collective-permute-start.10 = (bf16[1,32,6144]{2,1,0:T(8,128)(2,1)}, bf16[1,32,6144]{2,1,0:T(8,128)(2,1)}, u32[]{:S(2)}, u32[]{:S(2)}) collective-permute-start(bf16[1,32,6144]{2,1,0:T(8,128)(2,1)} %get-tuple-element.1516), channel_id=1, source_target_pairs={{0,4},{4,8},{8,12},{12,16},{16,20},{20,24},{24,28},{1,5},{5,9},{9,... | collective-permute-start | bytes 1179656 | tf_op jit(solution)/shard_map/while/body/eval_jaxpr/ppermute | solution.py:21
  230.7 2.6 collective-permute-done.11
  235.1 325.2 %while.62 = (s32[]{:T(128)}, bf16[4,32,6144]{2,1,0:T(8,128)(2,1)}, bf16[32,6144]{1,0:T(8,128)(2,1)}, f32[6144,128]{1,0:T(8,128)}, f32[128,6144]{1,0:T(8,128)}, /...) while((s32[]{:T(128)}, bf16[4,32,6144]{2,1,0:T(8,128)(2,1)}, ...), condition=%wide.region_45.46_spmd, body=%wide.region_30.45_spmd.sunk | while | flops 517882016 | bytes 62575540 | solution.py:134
  235.9 21.1 %collective-permute-start.4 = (bf16[1,32,6144]{2,1,0:T(8,128)(2,1)}, bf16[1,32,6144]{2,1,0:T(8,128)(2,1)}, u32[]{:S(2)}, u32[]{:S(2)}) collective-permute-start(bf16[1,32,6144]{2,1,0:T(8,128)(2,1)} %get-tuple-element.1786), channel_id=1, source_target_pairs={{0,4},{4,8},{8,12},{12,16},{16,20},{20,24},{24,28},{1,5},{5,9},{9,... | collective-permute-start | bytes 1179656 | tf_op jit(solution)/shard_map/while/body/eval_jaxpr/ppermute | solution.py:21
  258.4 12.4 %collective-permute-done.5 = bf16[1,32,6144]{2,1,0:T(8,128)(2,1)} collective-permute-done((bf16[1,32,6144]{2,1,0:T(8,128)(2,1)}, bf16[1,32,6144]{2,1,0:T(8,128)(2,1)}, u32[]{:S(2)}, u32[]{:S(2)}) %collective-permute-start.5) | collective-permute-done | bytes 393248 | tf_op jit(solution)/shard_map/while/body/eval_jaxpr/ppermute | solution.py:23
  273.4 30.8 %collective-permute-start.6 = (bf16[1,32,6144]{2,1,0:T(8,128)(2,1)}, bf16[1,32,6144]{2,1,0:T(8,128)(2,1)}, u32[]{:S(2)}, u32[]{:S(2)}) collective-permute-start(bf16[1,32,6144]{2,1,0:T(8,128)(2,1)} %get-tuple-element.1788), channel_id=1, source_target_pairs={{0,4},{4,8},{8,12},{12,16},{16,20},{20,24},{24,28},{1,5},{5,9},{9,... | collective-permute-start | bytes 1179656 | tf_op jit(solution)/shard_map/while/body/eval_jaxpr/ppermute | solution.py:21
  305.5 16.7 %collective-permute-done.7 = bf16[1,32,6144]{2,1,0:T(8,128)(2,1)} collective-permute-done((bf16[1,32,6144]{2,1,0:T(8,128)(2,1)}, bf16[1,32,6144]{2,1,0:T(8,128)(2,1)}, u32[]{:S(2)}, u32[]{:S(2)}) %collective-permute-start.7) | collective-permute-done | bytes 393248 | tf_op jit(solution)/shard_map/while/body/eval_jaxpr/ppermute | solution.py:23
  324.8 25.0 %collective-permute-start.4 = (bf16[1,32,6144]{2,1,0:T(8,128)(2,1)}, bf16[1,32,6144]{2,1,0:T(8,128)(2,1)}, u32[]{:S(2)}, u32[]{:S(2)}) collective-permute-start(bf16[1,32,6144]{2,1,0:T(8,128)(2,1)} %get-tuple-element.1786), channel_id=1, source_target_pairs={{0,4},{4,8},{8,12},{12,16},{16,20},{20,24},{24,28},{1,5},{5,9},{9,... | collective-permute-start | bytes 1179656 | tf_op jit(solution)/shard_map/while/body/eval_jaxpr/ppermute | solution.py:21
  355.5 16.2 %conditional.15 = (bf16[4,32,6144]{2,1,0:T(8,128)(2,1)}, f32[6144,128]{1,0:T(8,128)}, f32[128,6144]{1,0:T(8,128)}, f32[6144]{0:T(1024)S(1)}, bf16[1,32,6144]{2,1,0:T(8,128)(2,1)}) conditional(s32[]{:T(128)} %clamp.72, (bf16[4,32,6144]{2,1,0:T(8,128)(2,1)}, f32[6144,128]{1,0:T(8,128)}, f32[128,6144]{1,0:T(8,128)}, ...), branch_computations={%region_38.38_spmd, %region_39.40_spmd, %region_41.44_spmd} | conditional | flops 258744352 | bytes 26961444 | solution.py:104
  358.6 4.4 convolution_add_fusion.17
  363.0 4.8 convolution_add_fusion.16
  375.1 7.4 %collective-permute-done.7 = bf16[1,32,6144]{2,1,0:T(8,128)(2,1)} collective-permute-done((bf16[1,32,6144]{2,1,0:T(8,128)(2,1)}, bf16[1,32,6144]{2,1,0:T(8,128)(2,1)}, u32[]{:S(2)}, u32[]{:S(2)}) %collective-permute-start.7) | collective-permute-done | bytes 393248 | tf_op jit(solution)/shard_map/while/body/eval_jaxpr/ppermute | solution.py:23
  385.1 25.0 %collective-permute-start.4 = (bf16[1,32,6144]{2,1,0:T(8,128)(2,1)}, bf16[1,32,6144]{2,1,0:T(8,128)(2,1)}, u32[]{:S(2)}, u32[]{:S(2)}) collective-permute-start(bf16[1,32,6144]{2,1,0:T(8,128)(2,1)} %get-tuple-element.1786), channel_id=1, source_target_pairs={{0,4},{4,8},{8,12},{12,16},{16,20},{20,24},{24,28},{1,5},{5,9},{9,... | collective-permute-start | bytes 1179656 | tf_op jit(solution)/shard_map/while/body/eval_jaxpr/ppermute | solution.py:21
  415.8 16.2 %conditional.15 = (bf16[4,32,6144]{2,1,0:T(8,128)(2,1)}, f32[6144,128]{1,0:T(8,128)}, f32[128,6144]{1,0:T(8,128)}, f32[6144]{0:T(1024)S(1)}, bf16[1,32,6144]{2,1,0:T(8,128)(2,1)}) conditional(s32[]{:T(128)} %clamp.72, (bf16[4,32,6144]{2,1,0:T(8,128)(2,1)}, f32[6144,128]{1,0:T(8,128)}, f32[128,6144]{1,0:T(8,128)}, ...), branch_computations={%region_38.38_spmd, %region_39.40_spmd, %region_41.44_spmd} | conditional | flops 258744352 | bytes 26961444 | solution.py:104
  418.9 4.4 convolution_add_fusion.17
  423.3 4.8 convolution_add_fusion.16
  435.4 7.4 %collective-permute-done.7 = bf16[1,32,6144]{2,1,0:T(8,128)(2,1)} collective-permute-done((bf16[1,32,6144]{2,1,0:T(8,128)(2,1)}, bf16[1,32,6144]{2,1,0:T(8,128)(2,1)}, u32[]{:S(2)}, u32[]{:S(2)}) %collective-permute-start.7) | collective-permute-done | bytes 393248 | tf_op jit(solution)/shard_map/while/body/eval_jaxpr/ppermute | solution.py:23
  445.4 25.0 %collective-permute-start.4 = (bf16[1,32,6144]{2,1,0:T(8,128)(2,1)}, bf16[1,32,6144]{2,1,0:T(8,128)(2,1)}, u32[]{:S(2)}, u32[]{:S(2)}) collective-permute-start(bf16[1,32,6144]{2,1,0:T(8,128)(2,1)} %get-tuple-element.1786), channel_id=1, source_target_pairs={{0,4},{4,8},{8,12},{12,16},{16,20},{20,24},{24,28},{1,5},{5,9},{9,... | collective-permute-start | bytes 1179656 | tf_op jit(solution)/shard_map/while/body/eval_jaxpr/ppermute | solution.py:21
  476.1 16.2 %conditional.15 = (bf16[4,32,6144]{2,1,0:T(8,128)(2,1)}, f32[6144,128]{1,0:T(8,128)}, f32[128,6144]{1,0:T(8,128)}, f32[6144]{0:T(1024)S(1)}, bf16[1,32,6144]{2,1,0:T(8,128)(2,1)}) conditional(s32[]{:T(128)} %clamp.72, (bf16[4,32,6144]{2,1,0:T(8,128)(2,1)}, f32[6144,128]{1,0:T(8,128)}, f32[128,6144]{1,0:T(8,128)}, ...), branch_computations={%region_38.38_spmd, %region_39.40_spmd, %region_41.44_spmd} | conditional | flops 258744352 | bytes 26961444 | solution.py:104
  479.2 4.4 convolution_add_fusion.17
  483.6 4.8 convolution_add_fusion.16
  495.7 8.2 %collective-permute-done.7 = bf16[1,32,6144]{2,1,0:T(8,128)(2,1)} collective-permute-done((bf16[1,32,6144]{2,1,0:T(8,128)(2,1)}, bf16[1,32,6144]{2,1,0:T(8,128)(2,1)}, u32[]{:S(2)}, u32[]{:S(2)}) %collective-permute-start.7) | collective-permute-done | bytes 393248 | tf_op jit(solution)/shard_map/while/body/eval_jaxpr/ppermute | solution.py:23
  506.5 24.1 %collective-permute-start.4 = (bf16[1,32,6144]{2,1,0:T(8,128)(2,1)}, bf16[1,32,6144]{2,1,0:T(8,128)(2,1)}, u32[]{:S(2)}, u32[]{:S(2)}) collective-permute-start(bf16[1,32,6144]{2,1,0:T(8,128)(2,1)} %get-tuple-element.1786), channel_id=1, source_target_pairs={{0,4},{4,8},{8,12},{12,16},{16,20},{20,24},{24,28},{1,5},{5,9},{9,... | collective-permute-start | bytes 1179656 | tf_op jit(solution)/shard_map/while/body/eval_jaxpr/ppermute | solution.py:21
  536.3 16.2 %conditional.15 = (bf16[4,32,6144]{2,1,0:T(8,128)(2,1)}, f32[6144,128]{1,0:T(8,128)}, f32[128,6144]{1,0:T(8,128)}, f32[6144]{0:T(1024)S(1)}, bf16[1,32,6144]{2,1,0:T(8,128)(2,1)}) conditional(s32[]{:T(128)} %clamp.72, (bf16[4,32,6144]{2,1,0:T(8,128)(2,1)}, f32[6144,128]{1,0:T(8,128)}, f32[128,6144]{1,0:T(8,128)}, ...), branch_computations={%region_38.38_spmd, %region_39.40_spmd, %region_41.44_spmd} | conditional | flops 258744352 | bytes 26961444 | solution.py:104
  539.4 4.4 convolution_add_fusion.17
  543.8 4.8 convolution_add_fusion.16
  560.3 3.3 convert_element_type.216
  565.0 20.1 %psum.23 = bf16[1,6144]{1,0:T(2,128)(2,1)S(1)} all-reduce(bf16[1,6144]{1,0:T(2,128)(2,1)S(1)} %broadcast_in_dim.157), channel_id=1, replica_groups=mesh['pipe'=8,'dp'=4] {'dp'}, use_global_device_ids=true, to_apply=%region_48.49 | all-reduce | flops 6144 | bytes 24576 | tf_op jit(solution)/shard_map/psum | solution.py:154
  585.7 100.2 %all-reduce.3.cloned.1.call-done = (bf16[1,6144,128]{2,1,0:T(8,128)(2,1)}, bf16[1,128,6144]{2,1,0:T(8,128)(2,1)}) async-done(((bf16[1,6144,128]{2,1,0:T(8,128)(2,1)}, bf16[1,128,6144]{2,1,0:T(8,128)(2,1)}), (bf16[1,6144,128]{2,1,0:T(8,128)(2,1)}, bf16[1,128,6144]{2,1,0:T(8,128)(2,1)})) %all-reduce.3.cloned.1.call-update) | async-done | bytes 3145744 | tf_op jit(solution)/shard_map/psum | solution.py:152
  686.0 3.4 broadcast_in_dim.154
  (198 shorter events, 195.1 us)
Async XLA Ops:
  7.2 678.8 %all-reduce.3.cloned.1.call-start = ((), (), s32[]{:S(2)}) async-start(), calls=%async_computation | async-start | bytes 6291456 | tf_op jit(solution)/shard_map/psum | solution.py:152
  9.1 4.1 copy-start.1
  19.7 3.4 collective-permute-start
  21.8 3.9 collective-permute-start.1
  28.3 13.9 %collective-permute-start.2 = (bf16[1,32,6144]{2,1,0:T(8,128)(2,1)}, bf16[1,32,6144]{2,1,0:T(8,128)(2,1)}, u32[]{:S(2)}, u32[]{:S(2)}) collective-permute-start(bf16[1,32,6144]{2,1,0:T(8,128)(2,1)} %get-tuple-element.1766), channel_id=1, source_target_pairs={{0,4},{4,8},{8,12},{12,16},{16,20},{20,24},{24,28},{1,5},{5,9},{9,... | collective-permute-start | bytes 1179656 | tf_op jit(solution)/shard_map/while/body/eval_jaxpr/ppermute | solution.py:21
  40.9 3.9 collective-permute-start.3
  53.0 3.4 collective-permute-start
  55.0 8.0 %collective-permute-start.1 = (bf16[1,32,6144]{2,1,0:T(8,128)(2,1)}, bf16[1,32,6144]{2,1,0:T(8,128)(2,1)}, u32[]{:S(2)}, u32[]{:S(2)}) collective-permute-start(bf16[1,32,6144]{2,1,0:T(8,128)(2,1)} %get-tuple-element.1764), channel_id=1, source_target_pairs={{4,0},{8,4},{12,8},{16,12},{20,16},{24,20},{28,24},{5,1},{9,5},{13... | collective-permute-start | bytes 1179656 | tf_op jit(solution)/shard_map/while/body/eval_jaxpr/ppermute | solution.py:23
  65.6 15.7 %collective-permute-start.2 = (bf16[1,32,6144]{2,1,0:T(8,128)(2,1)}, bf16[1,32,6144]{2,1,0:T(8,128)(2,1)}, u32[]{:S(2)}, u32[]{:S(2)}) collective-permute-start(bf16[1,32,6144]{2,1,0:T(8,128)(2,1)} %get-tuple-element.1766), channel_id=1, source_target_pairs={{0,4},{4,8},{8,12},{12,16},{16,20},{20,24},{24,28},{1,5},{5,9},{9,... | collective-permute-start | bytes 1179656 | tf_op jit(solution)/shard_map/while/body/eval_jaxpr/ppermute | solution.py:21
  79.9 3.9 collective-permute-start.3
  92.0 3.4 collective-permute-start
  94.1 8.0 %collective-permute-start.1 = (bf16[1,32,6144]{2,1,0:T(8,128)(2,1)}, bf16[1,32,6144]{2,1,0:T(8,128)(2,1)}, u32[]{:S(2)}, u32[]{:S(2)}) collective-permute-start(bf16[1,32,6144]{2,1,0:T(8,128)(2,1)} %get-tuple-element.1764), channel_id=1, source_target_pairs={{4,0},{8,4},{12,8},{16,12},{20,16},{24,20},{28,24},{5,1},{9,5},{13... | collective-permute-start | bytes 1179656 | tf_op jit(solution)/shard_map/while/body/eval_jaxpr/ppermute | solution.py:23
  104.7 15.6 %collective-permute-start.2 = (bf16[1,32,6144]{2,1,0:T(8,128)(2,1)}, bf16[1,32,6144]{2,1,0:T(8,128)(2,1)}, u32[]{:S(2)}, u32[]{:S(2)}) collective-permute-start(bf16[1,32,6144]{2,1,0:T(8,128)(2,1)} %get-tuple-element.1766), channel_id=1, source_target_pairs={{0,4},{4,8},{8,12},{12,16},{16,20},{20,24},{24,28},{1,5},{5,9},{9,... | collective-permute-start | bytes 1179656 | tf_op jit(solution)/shard_map/while/body/eval_jaxpr/ppermute | solution.py:21
  119.0 3.9 collective-permute-start.3
  131.1 3.4 collective-permute-start
  133.2 8.0 %collective-permute-start.1 = (bf16[1,32,6144]{2,1,0:T(8,128)(2,1)}, bf16[1,32,6144]{2,1,0:T(8,128)(2,1)}, u32[]{:S(2)}, u32[]{:S(2)}) collective-permute-start(bf16[1,32,6144]{2,1,0:T(8,128)(2,1)} %get-tuple-element.1764), channel_id=1, source_target_pairs={{4,0},{8,4},{12,8},{16,12},{20,16},{24,20},{28,24},{5,1},{9,5},{13... | collective-permute-start | bytes 1179656 | tf_op jit(solution)/shard_map/while/body/eval_jaxpr/ppermute | solution.py:23
  143.7 15.8 %collective-permute-start.2 = (bf16[1,32,6144]{2,1,0:T(8,128)(2,1)}, bf16[1,32,6144]{2,1,0:T(8,128)(2,1)}, u32[]{:S(2)}, u32[]{:S(2)}) collective-permute-start(bf16[1,32,6144]{2,1,0:T(8,128)(2,1)} %get-tuple-element.1766), channel_id=1, source_target_pairs={{0,4},{4,8},{8,12},{12,16},{16,20},{20,24},{24,28},{1,5},{5,9},{9,... | collective-permute-start | bytes 1179656 | tf_op jit(solution)/shard_map/while/body/eval_jaxpr/ppermute | solution.py:21
  158.2 3.9 collective-permute-start.3
  164.8 9.7 %collective-permute-start = (bf16[1,32,6144]{2,1,0:T(8,128)(2,1)}, bf16[1,32,6144]{2,1,0:T(8,128)(2,1)}, u32[]{:S(2)}, u32[]{:S(2)}) collective-permute-start(bf16[1,32,6144]{2,1,0:T(8,128)(2,1)} %get-tuple-element.1764), channel_id=1, source_target_pairs={{0,4},{4,8},{8,12},{12,16},{16,20},{20,24},{24,28},{1,5},{5,9},{9,... | collective-permute-start | bytes 1179656 | tf_op jit(solution)/shard_map/while/body/eval_jaxpr/ppermute | solution.py:21
  173.0 8.3 %collective-permute-start.1 = (bf16[1,32,6144]{2,1,0:T(8,128)(2,1)}, bf16[1,32,6144]{2,1,0:T(8,128)(2,1)}, u32[]{:S(2)}, u32[]{:S(2)}) collective-permute-start(bf16[1,32,6144]{2,1,0:T(8,128)(2,1)} %get-tuple-element.1764), channel_id=1, source_target_pairs={{4,0},{8,4},{12,8},{16,12},{20,16},{24,20},{28,24},{5,1},{9,5},{13... | collective-permute-start | bytes 1179656 | tf_op jit(solution)/shard_map/while/body/eval_jaxpr/ppermute | solution.py:23
  183.9 10.8 %collective-permute-start.2 = (bf16[1,32,6144]{2,1,0:T(8,128)(2,1)}, bf16[1,32,6144]{2,1,0:T(8,128)(2,1)}, u32[]{:S(2)}, u32[]{:S(2)}) collective-permute-start(bf16[1,32,6144]{2,1,0:T(8,128)(2,1)} %get-tuple-element.1766), channel_id=1, source_target_pairs={{0,4},{4,8},{8,12},{12,16},{16,20},{20,24},{24,28},{1,5},{5,9},{9,... | collective-permute-start | bytes 1179656 | tf_op jit(solution)/shard_map/while/body/eval_jaxpr/ppermute | solution.py:21
  193.3 3.9 collective-permute-start.3
  199.8 15.6 %collective-permute-start.8 = (bf16[1,32,6144]{2,1,0:T(8,128)(2,1)}, bf16[1,32,6144]{2,1,0:T(8,128)(2,1)}, u32[]{:S(2)}, u32[]{:S(2)}) collective-permute-start(bf16[1,32,6144]{2,1,0:T(8,128)(2,1)} %get-tuple-element.1514), channel_id=1, source_target_pairs={{0,4},{4,8},{8,12},{12,16},{16,20},{20,24},{24,28},{1,5},{5,9},{9,... | collective-permute-start | bytes 1179656 | tf_op jit(solution)/shard_map/while/body/eval_jaxpr/ppermute | solution.py:21
  214.1 3.9 collective-permute-start.9
  220.6 10.1 %collective-permute-start.10 = (bf16[1,32,6144]{2,1,0:T(8,128)(2,1)}, bf16[1,32,6144]{2,1,0:T(8,128)(2,1)}, u32[]{:S(2)}, u32[]{:S(2)}) collective-permute-start(bf16[1,32,6144]{2,1,0:T(8,128)(2,1)} %get-tuple-element.1516), channel_id=1, source_target_pairs={{0,4},{4,8},{8,12},{12,16},{16,20},{20,24},{24,28},{1,5},{5,9},{9,... | collective-permute-start | bytes 1179656 | tf_op jit(solution)/shard_map/while/body/eval_jaxpr/ppermute | solution.py:21
  229.4 3.9 collective-permute-start.11
  235.9 22.5 %collective-permute-start.4 = (bf16[1,32,6144]{2,1,0:T(8,128)(2,1)}, bf16[1,32,6144]{2,1,0:T(8,128)(2,1)}, u32[]{:S(2)}, u32[]{:S(2)}) collective-permute-start(bf16[1,32,6144]{2,1,0:T(8,128)(2,1)} %get-tuple-element.1786), channel_id=1, source_target_pairs={{0,4},{4,8},{8,12},{12,16},{16,20},{20,24},{24,28},{1,5},{5,9},{9,... | collective-permute-start | bytes 1179656 | tf_op jit(solution)/shard_map/while/body/eval_jaxpr/ppermute | solution.py:21
  257.1 13.8 %collective-permute-start.5 = (bf16[1,32,6144]{2,1,0:T(8,128)(2,1)}, bf16[1,32,6144]{2,1,0:T(8,128)(2,1)}, u32[]{:S(2)}, u32[]{:S(2)}) collective-permute-start(bf16[1,32,6144]{2,1,0:T(8,128)(2,1)} %get-tuple-element.1786), channel_id=1, source_target_pairs={{4,0},{8,4},{12,8},{16,12},{20,16},{24,20},{28,24},{5,1},{9,5},{13... | collective-permute-start | bytes 1179656 | tf_op jit(solution)/shard_map/while/body/eval_jaxpr/ppermute | solution.py:23
  273.4 32.1 %collective-permute-start.6 = (bf16[1,32,6144]{2,1,0:T(8,128)(2,1)}, bf16[1,32,6144]{2,1,0:T(8,128)(2,1)}, u32[]{:S(2)}, u32[]{:S(2)}) collective-permute-start(bf16[1,32,6144]{2,1,0:T(8,128)(2,1)} %get-tuple-element.1788), channel_id=1, source_target_pairs={{0,4},{4,8},{8,12},{12,16},{16,20},{20,24},{24,28},{1,5},{5,9},{9,... | collective-permute-start | bytes 1179656 | tf_op jit(solution)/shard_map/while/body/eval_jaxpr/ppermute | solution.py:21
  304.2 18.0 %collective-permute-start.7 = (bf16[1,32,6144]{2,1,0:T(8,128)(2,1)}, bf16[1,32,6144]{2,1,0:T(8,128)(2,1)}, u32[]{:S(2)}, u32[]{:S(2)}) collective-permute-start(bf16[1,32,6144]{2,1,0:T(8,128)(2,1)} %get-tuple-element.1788), channel_id=1, source_target_pairs={{4,0},{8,4},{12,8},{16,12},{20,16},{24,20},{28,24},{5,1},{9,5},{13... | collective-permute-start | bytes 1179656 | tf_op jit(solution)/shard_map/while/body/eval_jaxpr/ppermute | solution.py:23
  324.8 26.3 %collective-permute-start.4 = (bf16[1,32,6144]{2,1,0:T(8,128)(2,1)}, bf16[1,32,6144]{2,1,0:T(8,128)(2,1)}, u32[]{:S(2)}, u32[]{:S(2)}) collective-permute-start(bf16[1,32,6144]{2,1,0:T(8,128)(2,1)} %get-tuple-element.1786), channel_id=1, source_target_pairs={{0,4},{4,8},{8,12},{12,16},{16,20},{20,24},{24,28},{1,5},{5,9},{9,... | collective-permute-start | bytes 1179656 | tf_op jit(solution)/shard_map/while/body/eval_jaxpr/ppermute | solution.py:21
  349.7 3.9 collective-permute-start.5
  371.7 3.4 collective-permute-start.6
  373.8 8.7 %collective-permute-start.7 = (bf16[1,32,6144]{2,1,0:T(8,128)(2,1)}, bf16[1,32,6144]{2,1,0:T(8,128)(2,1)}, u32[]{:S(2)}, u32[]{:S(2)}) collective-permute-start(bf16[1,32,6144]{2,1,0:T(8,128)(2,1)} %get-tuple-element.1788), channel_id=1, source_target_pairs={{4,0},{8,4},{12,8},{16,12},{20,16},{24,20},{28,24},{5,1},{9,5},{13... | collective-permute-start | bytes 1179656 | tf_op jit(solution)/shard_map/while/body/eval_jaxpr/ppermute | solution.py:23
  385.1 26.4 %collective-permute-start.4 = (bf16[1,32,6144]{2,1,0:T(8,128)(2,1)}, bf16[1,32,6144]{2,1,0:T(8,128)(2,1)}, u32[]{:S(2)}, u32[]{:S(2)}) collective-permute-start(bf16[1,32,6144]{2,1,0:T(8,128)(2,1)} %get-tuple-element.1786), channel_id=1, source_target_pairs={{0,4},{4,8},{8,12},{12,16},{16,20},{20,24},{24,28},{1,5},{5,9},{9,... | collective-permute-start | bytes 1179656 | tf_op jit(solution)/shard_map/while/body/eval_jaxpr/ppermute | solution.py:21
  410.0 3.9 collective-permute-start.5
  432.0 3.4 collective-permute-start.6
  434.1 8.7 %collective-permute-start.7 = (bf16[1,32,6144]{2,1,0:T(8,128)(2,1)}, bf16[1,32,6144]{2,1,0:T(8,128)(2,1)}, u32[]{:S(2)}, u32[]{:S(2)}) collective-permute-start(bf16[1,32,6144]{2,1,0:T(8,128)(2,1)} %get-tuple-element.1788), channel_id=1, source_target_pairs={{4,0},{8,4},{12,8},{16,12},{20,16},{24,20},{28,24},{5,1},{9,5},{13... | collective-permute-start | bytes 1179656 | tf_op jit(solution)/shard_map/while/body/eval_jaxpr/ppermute | solution.py:23
  445.4 26.4 %collective-permute-start.4 = (bf16[1,32,6144]{2,1,0:T(8,128)(2,1)}, bf16[1,32,6144]{2,1,0:T(8,128)(2,1)}, u32[]{:S(2)}, u32[]{:S(2)}) collective-permute-start(bf16[1,32,6144]{2,1,0:T(8,128)(2,1)} %get-tuple-element.1786), channel_id=1, source_target_pairs={{0,4},{4,8},{8,12},{12,16},{16,20},{20,24},{24,28},{1,5},{5,9},{9,... | collective-permute-start | bytes 1179656 | tf_op jit(solution)/shard_map/while/body/eval_jaxpr/ppermute | solution.py:21
  470.4 3.9 collective-permute-start.5
  492.3 3.4 collective-permute-start.6
  494.4 9.5 %collective-permute-start.7 = (bf16[1,32,6144]{2,1,0:T(8,128)(2,1)}, bf16[1,32,6144]{2,1,0:T(8,128)(2,1)}, u32[]{:S(2)}, u32[]{:S(2)}) collective-permute-start(bf16[1,32,6144]{2,1,0:T(8,128)(2,1)} %get-tuple-element.1788), channel_id=1, source_target_pairs={{4,0},{8,4},{12,8},{16,12},{20,16},{24,20},{28,24},{5,1},{9,5},{13... | collective-permute-start | bytes 1179656 | tf_op jit(solution)/shard_map/while/body/eval_jaxpr/ppermute | solution.py:23
  506.5 25.4 %collective-permute-start.4 = (bf16[1,32,6144]{2,1,0:T(8,128)(2,1)}, bf16[1,32,6144]{2,1,0:T(8,128)(2,1)}, u32[]{:S(2)}, u32[]{:S(2)}) collective-permute-start(bf16[1,32,6144]{2,1,0:T(8,128)(2,1)} %get-tuple-element.1786), channel_id=1, source_target_pairs={{0,4},{4,8},{8,12},{12,16},{16,20},{20,24},{24,28},{1,5},{5,9},{9,... | collective-permute-start | bytes 1179656 | tf_op jit(solution)/shard_map/while/body/eval_jaxpr/ppermute | solution.py:21
  530.6 3.9 collective-permute-start.5
  552.5 3.4 collective-permute-start.6
  554.6 3.9 collective-permute-start.7
  560.3 3.3 copy-start.2
  686.0 3.4 copy-start.16
  (10 other events, 14.6 us)
Sparse Core Ops, SparseCore 0:
  565.1 120.8 all-reduce.2
where the time goes:
time: 701 us; the launch traced here: 698 us
  starting transfers between devices  292 us (42%)
  waiting for transfers between devices  213 us (30%)
  other arithmetic  75.4 us (11%)
  matrix products  57 us (8%)
  local copies, waits for them, and re-layouts  24.5 us (3%)
  blocking collectives  20.1 us (3%)
  between operations  14.2 us (2%)
    ppermute x22, starting transfers between devices, with_halo(): lax.ppermute(tail, axis, [(i, (i + 1) % count) for i in range(ends)])  264 us
    ppermute x22, waiting for transfers between devices, with_halo(): lax.ppermute(head, axis, [((i + 1) % count, i) for i in range(ends)])  113 us
    psum x1, waiting for transfers between devices, per_device(): lax.psum(low_parts[0].astype(jnp.float32).astype(jnp.bfloat16), 'dp')  100 us
    select_n x22, other arithmetic, pass_along(): return jnp.where(forward_next, padded[0], padded[2])  39.2 us
    ppermute x22, starting transfers between devices, with_halo(): lax.ppermute(head, axis, [((i + 1) % count, i) for i in range(ends)])  28.2 us
    psum x1, blocking collectives, per_device(): lax.psum(low_parts[2].astype(jnp.float32).astype(jnp.bfloat16), 'dp')  20.1 us
    dot_general x4, matrix products, backward_turn(): jnp.einsum('tk,tj->kj', values, upstream, preferred_element_type=jnp.floa...  19.2 us
    dot_general x4, matrix products, backward_turn(): jnp.einsum('td,tk->dk', mixed_rows, dvalues, preferred_element_type=jnp.f...  17.6 us
  transfers between devices with their start and end apart: 45, of which 23 were waited for; matrix products, arithmetic and copies ran while one was open for 0% of the time, Pallas kernels for 0%

commit v1 on v0

v1 whole, which is shorter than its diff:
```python
import functools

import jax
import jax.numpy as jnp
from jax import lax
from jax.experimental import pallas as pl
from jax.experimental.pallas import tpu as pltpu
from jax.sharding import PartitionSpec as P

epsilon = 1e-05
MESH = pl.DeviceIdType.MESH
F32 = jnp.float32
BF16 = jnp.bfloat16
TAIL = 16


def dot(a, b, dims):
    return lax.dot_general(a, b, (dims, ((), ())), preferred_element_type=F32)


def split_rows(row):
    wide = jnp.broadcast_to(row, (TAIL, row.shape[-1]))
    high = wide.astype(BF16).astype(F32)
    at = lax.broadcasted_iota(jnp.int32, wide.shape, 0)
    return jnp.where(at < 8, high, wide - high).astype(BF16)


def joined_row(tail):
    tail = tail.astype(F32)
    return tail[0:1] + tail[8:9]


def as_column(row, lanes):
    return jnp.broadcast_to(row, (lanes, row.shape[-1])).T


def kernel(
    n_pipe, n_dp,
    gains, inputs, cotangent, w_value, w_out,
    gv_out, go_out, gg_out,
    wv_all, wo_all, ga_all, h0_all, cot_all, own_h, vq, xs, xbuf,
    h_all, g_all, g_own, acc_v, acc_o, acc_g, gs_v, gs_o, gs_g,
    w_send, w_recv, in_send, in_recv, x_send, x_recv,
    v_send, v_recv, d_send, d_recv, o_send, o_recv,
):
    me = lax.axis_index("pipe")
    z = lax.axis_index("dp")
    layers = n_pipe
    width = wv_all.shape[1]
    full = width * n_pipe
    rank = wv_all.shape[2]
    tokens = own_h.shape[1]

    def plane_peer(k):
        return lax.rem(me + k, n_pipe)

    def line_peer(k):
        return lax.rem(z + k, n_dp)

    barrier = pltpu.get_barrier_semaphore()
    for k in range(1, n_pipe):
        pl.semaphore_signal(barrier, inc=1, device_id=(plane_peer(k), z), device_id_type=MESH)
    for k in range(1, n_dp):
        pl.semaphore_signal(barrier, inc=1, device_id=(me, line_peer(k)), device_id_type=MESH)
    pl.semaphore_wait(barrier, n_pipe + n_dp - 2)

    def columns(owner):
        return pl.ds(pl.multiple_of(owner * width, width), width)

    def remote(src, dst, send, recv, to):
        return pltpu.make_async_remote_copy(
            src_ref=src, dst_ref=dst, send_sem=send, recv_sem=recv, device_id=to, device_id_type=MESH
        )

    def wait_local(dst, sem):
        pltpu.make_async_copy(dst, dst, sem).wait()

    pltpu.make_async_copy(inputs.at[:, :, columns(me)], h0_all.at[z], in_recv.at[0, 0]).start()
    pltpu.make_async_copy(cotangent.at[:, :, columns(me)], cot_all.at[z], in_recv.at[1, 0]).start()
    pltpu.make_async_copy(gains.at[:, columns(me)], ga_all.at[me], w_recv.at[0, me]).start()
    pltpu.make_async_copy(w_value.at[columns(me), :], wv_all.at[me], w_recv.at[1, me]).start()
    pltpu.make_async_copy(w_out.at[:, columns(me)], wo_all.at[me], w_recv.at[2, me]).start()

    def weight_copies(k):
        d = plane_peer(k)
        return (
            remote(gains.at[:, columns(d)], ga_all.at[me], w_send.at[0, k], w_recv.at[0, me], (d, z)),
            remote(w_value.at[columns(d), :], wv_all.at[me], w_send.at[1, k], w_recv.at[1, me], (d, z)),
            remote(w_out.at[:, columns(d)], wo_all.at[me], w_send.at[2, k], w_recv.at[2, me], (d, z)),
        )

    def input_copies(k):
        d = line_peer(k)
        return (
            remote(inputs.at[:, :, columns(me)], h0_all.at[z], in_send.at[0, k], in_recv.at[0, k], (me, d)),
            remote(cotangent.at[:, :, columns(me)], cot_all.at[z], in_send.at[1, k], in_recv.at[1, k], (me, d)),
        )

    def line_copies(buf, send, recv, s):
        return [
            remote(buf.at[s, z], buf.at[s, z], send.at[s, k], recv.at[s, k], (me, line_peer(k)))
            for k in range(1, n_dp)
        ]

    def exchange_copies(slot, rows):
        return [
            remote(
                xbuf.at[slot, 0, pl.ds(0, rows)], xbuf.at[slot, k, pl.ds(0, rows)],
                x_send.at[slot, k], x_recv.at[slot, k], (plane_peer(k), z),
            )
            for k in range(1, n_pipe)
        ]

    for k in range(1, n_pipe):
        for copy in weight_copies(k):
            copy.start()
    for k in range(1, n_dp):
        for copy in input_copies(k):
            copy.start()

    wait_local(h0_all.at[z], in_recv.at[0, 0])
    wait_local(cot_all.at[z], in_recv.at[1, 0])
    own_h[0] = h0_all[z].reshape(tokens, width)
    g_own[...] = cot_all[z].reshape(tokens, width).astype(F32)

    def forward(s, carry):
        slot = lax.rem(s, 2)
        wait_local(ga_all.at[s], w_recv.at[0, s])
        wait_local(wv_all.at[s], w_recv.at[1, s])
        floats = own_h[s].astype(F32)
        scaled = (floats * ga_all[s, 0:1, :]).astype(BF16)
        part = dot(scaled, wv_all[s], ((1,), (0,)))
        squares = dot(jnp.ones((8, width), BF16), (floats * floats).astype(BF16), ((1,), (1,)))
        xbuf[slot, 0, 0:tokens, :] = part.astype(BF16)
        xbuf[slot, 0, tokens:, :] = split_rows(squares[0:1])
        copies = exchange_copies(slot, tokens + TAIL)
        for copy in copies:
            copy.start()
        wait_local(wo_all.at[s], w_recv.at[2, s])
        row = joined_row(xbuf[slot, 0, tokens:, :])
        total = part
        for k, copy in enumerate(copies, 1):
            copy.wait_recv()
            total = total + xbuf[slot, k, 0:tokens, :].astype(F32)
            row = row + joined_row(xbuf[slot, k, tokens:, :])
        scale = lax.rsqrt(row * (1.0 / full) + epsilon)
        values = (total * as_column(scale, rank)).astype(BF16)
        vq[s, z, 0:tokens, :] = values
        vq[s, z, tokens:, :] = split_rows(scale)
        for copy in line_copies(vq, v_send, v_recv, s):
            copy.start()
        own_h[s + 1] = (floats + dot(values, wo_all[s], ((1,), (0,)))).astype(BF16)
        for copy in copies:
            copy.wait_send()
        return carry

    lax.fori_loop(0, layers, forward, 0)

    def fill_all():
        for k in range(1, n_dp):
            for copy in input_copies(k):
                copy.wait()

        def arrive(s, carry):
            for copy in line_copies(vq, v_send, v_recv, s):
                copy.wait()
            return carry

        lax.fori_loop(0, layers, arrive, 0)

        def replica(r, carry):
            g_all[r] = cot_all[r].reshape(tokens, width).astype(F32)
            h_all[r] = h0_all[r].reshape(tokens, width).astype(F32)

            def add(s, inner):
                h_all[r] += dot(vq[s, r, 0:tokens, :], wo_all[s], ((1,), (0,)))
                return inner

            lax.fori_loop(0, layers, add, 0)
            return carry

        lax.fori_loop(0, n_dp, replica, 0)

    def gradients(s):
        for copy in line_copies(xs, d_send, d_recv, s):
            copy.wait()
        acc_v[...] = jnp.zeros_like(acc_v)
        acc_o[...] = jnp.zeros_like(acc_o)
        acc_g[...] = jnp.zeros_like(acc_g)

        def replica(r, carry):
            gain = ga_all[s, 0:1, :]
            values = vq[s, r, 0:tokens, :]
            scale = as_column(joined_row(vq[s, r, tokens:, :]), rank)
            scaled_dv = xs[s, r]
            floats = h_all[r] - dot(values, wo_all[s], ((1,), (0,)))
            h_all[r] = floats
            upper = g_all[r]
            acc_o[...] += dot(values, upper.astype(BF16), ((0,), (0,)))
            acc_v[...] += dot((floats * gain).astype(BF16), scaled_dv, ((0,), (0,)))
            du = dot(scaled_dv, wv_all[s], ((1,), (1,)))
            acc_g[0:1, :] += jnp.sum(du * floats, axis=0, keepdims=True)
            weigh = jnp.sum(scaled_dv.astype(F32) * values.astype(F32) * scale, axis=1, keepdims=True)
            g_all[r] = upper + (du * gain - floats * (weigh * (1.0 / full)))
            return carry

        lax.fori_loop(0, n_dp, replica, 0)
        gs_v[s] = acc_v[...].astype(BF16)
        gs_o[s] = acc_o[...].astype(BF16)
        gs_g[s] = acc_g[...]

        @pl.when(s == me)
        def _():
            pltpu.make_async_copy(gs_v.at[s], gv_out.at[me], o_recv.at[0, me]).start()
            pltpu.make_async_copy(gs_o.at[s], go_out.at[:, columns(me)], o_recv.at[1, me]).start()
            pltpu.make_async_copy(gs_g.at[s], gg_out.at[me], o_recv.at[2, me]).start()

        @pl.when(s != me)
        def _():
            remote(gs_v.at[s], gv_out.at[me], o_send.at[0, s], o_recv.at[0, me], (s, z)).start()
            remote(gs_o.at[s], go_out.at[:, columns(me)], o_send.at[1, s], o_recv.at[1, me], (s, z)).start()
            remote(gs_g.at[s], gg_out.at[me], o_send.at[2, s], o_recv.at[2, me], (s, z)).start()

    def backward(i, carry):
        s = layers - 1 - i
        slot = lax.rem(layers + i, 2)
        upper = g_own[...]
        part = dot(upper.astype(BF16), wo_all[s], ((1,), (1,)))
        xbuf[slot, 0, 0:tokens, :] = part.astype(BF16)
        copies = exchange_copies(slot, tokens)
        for copy in copies:
            copy.start()

        @pl.when(i == 0)
        def _():
            fill_all()

        @pl.when(i > 0)
        def _():
            gradients(s + 1)

        total = part
        for k, copy in enumerate(copies, 1):
            copy.wait_recv()
            total = total + xbuf[slot, k, 0:tokens, :].astype(F32)
        scale = as_column(joined_row(vq[s, z, tokens:, :]), rank)
        scaled_dv = (total * scale).astype(BF16)
        xs[s, z] = scaled_dv
        for copy in line_copies(xs, d_send, d_recv, s):
            copy.start()
        values = vq[s, z, 0:tokens, :].astype(F32)
        weigh = jnp.sum(scaled_dv.astype(F32) * values * scale, axis=1, keepdims=True)
        du = dot(scaled_dv, wv_all[s], ((1,), (1,)))
        floats = own_h[s].astype(F32)
        g_own[...] = upper + (du * ga_all[s, 0:1, :] - floats * (weigh * (1.0 / full)))
        for copy in copies:
            copy.wait_send()
        return carry

    lax.fori_loop(0, layers, backward, 0)
    gradients(0)

    for k in range(1, n_pipe):
        for copy in weight_copies(k):
            copy.wait_send()

    def finish(s, carry):
        wait_local(gv_out.at[s], o_recv.at[0, s])
        wait_local(go_out.at[:, columns(s)], o_recv.at[1, s])
        wait_local(gg_out.at[s], o_recv.at[2, s])

        @pl.when(s != me)
        def _():
            remote(gs_v.at[s], gv_out.at[me], o_send.at[0, s], o_recv.at[0, me], (s, z)).wait_send()
            remote(gs_o.at[s], go_out.at[:, columns(me)], o_send.at[1, s], o_recv.at[1, me], (s, z)).wait_send()
            remote(gs_g.at[s], gg_out.at[me], o_send.at[2, s], o_recv.at[2, me], (s, z)).wait_send()

        return carry

    lax.fori_loop(0, n_pipe, finish, 0)


def per_device(n_pipe, n_dp, inputs, cotangent, gains, w_value, w_out):
    batches, rows, full = inputs.shape
    rank = w_value.shape[-1]
    width = full // n_pipe
    tokens = batches * rows
    layers = n_pipe
    any_spec = pl.BlockSpec(memory_space=pl.ANY)
    dma = pltpu.SemaphoreType.DMA
    gv, go, gg = pl.pallas_call(
        functools.partial(kernel, n_pipe, n_dp),
        out_shape=(
            jax.ShapeDtypeStruct((n_pipe, width, rank), BF16),
            jax.ShapeDtypeStruct((rank, full), BF16),
            jax.ShapeDtypeStruct((n_pipe, 8, width), F32),
        ),
        in_specs=[any_spec] * 5,
        out_specs=(any_spec,) * 3,
        scratch_shapes=[
            pltpu.VMEM((layers, width, rank), BF16),
            pltpu.VMEM((layers, rank, width), BF16),
            pltpu.VMEM((layers, 8, width), F32),
            pltpu.VMEM((n_dp, batches, rows, width), BF16),
            pltpu.VMEM((n_dp, batches, rows, width), BF16),
            pltpu.VMEM((layers + 1, tokens, width), BF16),
            pltpu.VMEM((layers, n_dp, tokens + TAIL, rank), BF16),
            pltpu.VMEM((layers, n_dp, tokens, rank), BF16),
            pltpu.VMEM((2, n_pipe, tokens + TAIL, rank), BF16),
            pltpu.VMEM((n_dp, tokens, width), F32),
            pltpu.VMEM((n_dp, tokens, width), F32),
            pltpu.VMEM((tokens, width), F32),
            pltpu.VMEM((width, rank), F32),
            pltpu.VMEM((rank, width), F32),
            pltpu.VMEM((8, width), F32),
            pltpu.VMEM((layers, width, rank), BF16),
            pltpu.VMEM((layers, rank, width), BF16),
            pltpu.VMEM((layers, 8, width), F32),
            dma((3, n_pipe)), dma((3, n_pipe)),
            dma((2, n_dp)), dma((2, n_dp)),
            dma((2, n_pipe)), dma((2, n_pipe)),
            dma((layers, n_dp)), dma((layers, n_dp)),
            dma((layers, n_dp)), dma((layers, n_dp)),
            dma((3, n_pipe)), dma((3, n_pipe)),
        ],
        compiler_params=pltpu.CompilerParams(
            collective_id=0, has_side_effects=True, vmem_limit_bytes=56 * 1024 * 1024
        ),
        cost_estimate=pl.CostEstimate(
            flops=40 * n_dp * tokens * full * rank, bytes_accessed=16 * full * rank, transcendentals=0
        ),
    )(jnp.broadcast_to(gains, (8, full)), inputs, cotangent, w_value[0], w_out[0])
    return (
        gv.reshape(1, full, rank).astype(F32),
        go[None].astype(F32),
        gg[:, 0, :].reshape(1, full),
    )


def solution(mesh):
    placed = (
        P(None, "dp", None),
        P(None, "dp", None),
        P("pipe", None),
        P("pipe", None, None),
        P("pipe", None, None),
    )
    return jax.shard_map(
        functools.partial(per_device, mesh.shape["pipe"], mesh.shape["dp"]),
        mesh=mesh,
        in_specs=placed,
        out_specs=(P("pipe", None, None), P("pipe", None, None), P("pipe", None)),
        check_vma=False,
    )
```

time: 701 us -> 235 us (0.34)
  starting transfers between devices: 292 us -> 0 us
  Pallas kernels: 0 us -> 226 us
  waiting for transfers between devices: 213 us -> 0 us
  other arithmetic: 75.4 us -> 5.37 us
  matrix products: 57 us -> 0 us
  local copies, waits for them, and re-layouts: 24.5 us -> 2.98 us
  blocking collectives: 20.1 us -> 0 us
  between operations: 14.2 us -> 0.64 us
    ppermute x44 -> x0, starting transfers between devices: 292 us -> none  [the longest x22 264 us: with_halo(): lax.ppermute(tail, axis, [(i, (i + 1) % count) for i in range(ends)])]
    pallas_call x0 -> x1, Pallas kernels: none -> 226 us  [per_device(): pl.pallas_call(functools.partial(kernel, n_pipe, n_dp), out_shape=(jax.Sh...]
    ppermute x44 -> x0, waiting for transfers between devices: 113 us -> none  [the longest x22 113 us: with_halo(): lax.ppermute(head, axis, [((i + 1) % count, i) for i in range(ends)])]
    psum x1 -> x0, waiting for transfers between devices: 100 us -> none  [per_device(): lax.psum(low_parts[0].astype(jnp.float32).astype(jnp.bfloat16), 'dp')]
    dot_general x20 -> x0, matrix products: 57 us -> none  [the longest x4 19.2 us: backward_turn(): jnp.einsum('tk,tj->kj', values, upstream, preferred_element_type=jnp.floa...]
    select_n x26 -> x0, other arithmetic: 43.8 us -> none  [the longest x22 39.2 us: pass_along(): return jnp.where(forward_next, padded[0], padded[2])]
    psum x1 -> x0, blocking collectives: 20.1 us -> none  [per_device(): lax.psum(low_parts[2].astype(jnp.float32).astype(jnp.bfloat16), 'dp')]
    broadcast_in_dim x19 -> x1, local copies, waits for them, and re-layouts: 16.1 us -> 1.43 us  [per_device(): jnp.broadcast_to(gains, (8, full))]
  transfers between devices with their start and end apart: 45 -> 0, of which waited for: 23 -> 0; matrix products, arithmetic and copies ran while one was open for 0% -> 0% of each run, Pallas kernels for 0% -> 0%
where the time goes in v1:
time: 235 us
  Pallas kernels  226 us (96%)
  other arithmetic  5.37 us (2%)
  local copies, waits for them, and re-layouts  2.98 us (1%)
    pallas_call x1, Pallas kernels, per_device(): pl.pallas_call(functools.partial(kernel, n_pipe, n_dp), out_shape=(jax.Sh...  226 us

profile of v1, /device:TPU:0, one launch (start us, length us, event | category | flops | bytes accessed | tf_op | source)
XLA Modules:
  0.0 234.8 jit_solution(15151785338108168581)
XLA Ops:
  0.6 1.4 broadcast_in_dim.9.gains
  2.1 225.8 %shard_map.76 = (bf16[8,768,128]{2,1,0:T(8,128)(2,1)}, bf16[128,6144]{1,0:T(8,128)(2,1)}, f32[8,8,768]{2,1,0:T(8,128)}) custom-call(f32[8,6144]{1,0:T(8,128)} %broadcast_in_dim.9.gains, bf16[4,32,6144]{2,1,0:T(8,128)(2,1)} %inputs.1, bf16[4,32,6144]{2,1,0:T(8,128)(2,1)} %cotangent.1, bf16[6144,128]{1,0:T(8,128)(2,1)} %bitcast.14, bf16[128,6144]{1,0:T(8,128)(2,1)} %bitcast.15), custom_call_target="tpu_custom_call" | custom-call | flops 16106127360 | bytes 12582912 | tf_op jit(solution)/shard_map/pallas_call | solution.py:291
  227.9 1.5 slice.3
  229.4 0.0 copy-start
  229.4 3.4 %bitcast_convert_fusion.1 = f32[1,6144,128]{2,1,0:T(8,128)} fusion(bf16[1,6144,128]{2,1,0:T(8,128)(2,1)} %bitcast.11), kind=kLoop, calls=%fused_computation.1 | loop fusion | flops 786432 | bytes 4718592 | tf_op jit(solution)/shard_map/convert_element_type | solution.py:334
  232.8 0.0 copy-done
  232.8 2.0 bitcast_convert_fusion
Async XLA Ops:
  229.4 3.4 %copy-start = (bf16[128,6144]{1,0:T(8,128)(2,1)S(1)}, bf16[128,6144]{1,0:T(8,128)(2,1)}, u32[]{:S(2)}) copy-start(bf16[128,6144]{1,0:T(8,128)(2,1)} %get-tuple-element.7) | copy-start | bytes 4718596

commit v2 on v1

--- a/solution.py
+++ b/solution.py
@@ -209,6 +209,7 @@
         gs_o[s] = acc_o[...].astype(BF16)
         gs_g[s] = acc_g[...]
 
+    def send_out(s):
         @pl.when(s == me)
         def _():
             pltpu.make_async_copy(gs_v.at[s], gv_out.at[me], o_recv.at[0, me]).start()
@@ -259,6 +260,12 @@
 
     lax.fori_loop(0, layers, backward, 0)
     gradients(0)
+
+    def send_all(k, carry):
+        send_out(lax.rem(me + k, n_pipe))
+        return carry
+
+    lax.fori_loop(0, n_pipe, send_all, 0)
 
     for k in range(1, n_pipe):
         for copy in weight_copies(k):

time: 235 us -> 194 us (0.83)
  Pallas kernels: 226 us -> 184 us
    pallas_call x1, Pallas kernels: 226 us -> 184 us  [per_device(): pl.pallas_call(functools.partial(kernel, n_pipe, n_dp), out_shape=(jax.Sh...]
where the time goes in v2:
time: 194 us; the launch traced here: 193 us
  Pallas kernels  184 us (95%)
  other arithmetic  5.37 us (3%)
  local copies, waits for them, and re-layouts  2.98 us (2%)
    pallas_call x1, Pallas kernels, per_device(): pl.pallas_call(functools.partial(kernel, n_pipe, n_dp), out_shape=(jax.Sh...  184 us

profile of v2, /device:TPU:0, one launch (start us, length us, event | category | flops | bytes accessed | tf_op | source)
XLA Modules:
  0.0 192.7 jit_solution(12330348809309051346)
XLA Ops:
  0.6 1.4 broadcast_in_dim.9.gains
  2.1 183.8 %shard_map.76 = (bf16[8,768,128]{2,1,0:T(8,128)(2,1)}, bf16[128,6144]{1,0:T(8,128)(2,1)}, f32[8,8,768]{2,1,0:T(8,128)}) custom-call(f32[8,6144]{1,0:T(8,128)} %broadcast_in_dim.9.gains, bf16[4,32,6144]{2,1,0:T(8,128)(2,1)} %inputs.1, bf16[4,32,6144]{2,1,0:T(8,128)(2,1)} %cotangent.1, bf16[6144,128]{1,0:T(8,128)(2,1)} %bitcast.14, bf16[128,6144]{1,0:T(8,128)(2,1)} %bitcast.15), custom_call_target="tpu_custom_call" | custom-call | flops 16106127360 | bytes 12582912 | tf_op jit(solution)/shard_map/pallas_call | solution.py:298
  185.8 1.5 slice.3
  187.4 0.0 copy-start
  187.4 3.4 %bitcast_convert_fusion.1 = f32[1,6144,128]{2,1,0:T(8,128)} fusion(bf16[1,6144,128]{2,1,0:T(8,128)(2,1)} %bitcast.11), kind=kLoop, calls=%fused_computation.1 | loop fusion | flops 786432 | bytes 4718592 | tf_op jit(solution)/shard_map/convert_element_type | solution.py:341
  190.8 0.0 copy-done
  190.8 2.0 %bitcast_convert_fusion = f32[1,128,6144]{2,1,0:T(8,128)} fusion(bf16[128,6144]{1,0:T(8,128)(2,1)S(1)} %copy-done), kind=kLoop, calls=%fused_computation | loop fusion | flops 786432 | bytes 4718592 | tf_op jit(solution)/shard_map/convert_element_type | solution.py:342
Async XLA Ops:
  187.4 3.4 %copy-start = (bf16[128,6144]{1,0:T(8,128)(2,1)S(1)}, bf16[128,6144]{1,0:T(8,128)(2,1)}, u32[]{:S(2)}) copy-start(bf16[128,6144]{1,0:T(8,128)(2,1)} %get-tuple-element.7) | copy-start | bytes 4718596

commit v3 on v2

--- a/solution.py
+++ b/solution.py
@@ -300,14 +300,14 @@
         out_shape=(
             jax.ShapeDtypeStruct((n_pipe, width, rank), BF16),
             jax.ShapeDtypeStruct((rank, full), BF16),
-            jax.ShapeDtypeStruct((n_pipe, 8, width), F32),
+            jax.ShapeDtypeStruct((n_pipe, 1, width), F32),
         ),
         in_specs=[any_spec] * 5,
         out_specs=(any_spec,) * 3,
         scratch_shapes=[
             pltpu.VMEM((layers, width, rank), BF16),
             pltpu.VMEM((layers, rank, width), BF16),
-            pltpu.VMEM((layers, 8, width), F32),
+            pltpu.VMEM((layers, 1, width), F32),
             pltpu.VMEM((n_dp, batches, rows, width), BF16),
             pltpu.VMEM((n_dp, batches, rows, width), BF16),
             pltpu.VMEM((layers + 1, tokens, width), BF16),
@@ -319,10 +319,10 @@
             pltpu.VMEM((tokens, width), F32),
             pltpu.VMEM((width, rank), F32),
             pltpu.VMEM((rank, width), F32),
-            pltpu.VMEM((8, width), F32),
+            pltpu.VMEM((1, width), F32),
             pltpu.VMEM((layers, width, rank), BF16),
             pltpu.VMEM((layers, rank, width), BF16),
-            pltpu.VMEM((layers, 8, width), F32),
+            pltpu.VMEM((layers, 1, width), F32),
             dma((3, n_pipe)), dma((3, n_pipe)),
             dma((2, n_dp)), dma((2, n_dp)),
             dma((2, n_pipe)), dma((2, n_pipe)),
@@ -336,11 +336,11 @@
         cost_estimate=pl.CostEstimate(
             flops=40 * n_dp * tokens * full * rank, bytes_accessed=16 * full * rank, transcendentals=0
         ),
-    )(jnp.broadcast_to(gains, (8, full)), inputs, cotangent, w_value[0], w_out[0])
+    )(gains, inputs, cotangent, w_value[0], w_out[0])
     return (
         gv.reshape(1, full, rank).astype(F32),
         go[None].astype(F32),
-        gg[:, 0, :].reshape(1, full),
+        gg.reshape(1, full),
     )
 
 

time: 194 us -> 189 us (0.974)
  Pallas kernels: 184 us -> 181 us
  local copies, waits for them, and re-layouts: 2.98 us -> 0.62 us
    pallas_call x1, Pallas kernels: 184 us -> 181 us  [per_device(): pl.pallas_call(functools.partial(kernel, n_pipe, n_dp), out_shape=(jax.Sh...]
where the time goes in v3:
time: 189 us; the launch traced here: 187 us
  Pallas kernels  181 us (96%)
  other arithmetic  5.37 us (3%)
    pallas_call x1, Pallas kernels, per_device(): pl.pallas_call(functools.partial(kernel, n_pipe, n_dp), out_shape=(jax.Sh...  181 us

profile of v3, /device:TPU:0, one launch (start us, length us, event | category | flops | bytes accessed | tf_op | source)
XLA Modules:
  0.0 187.5 jit_solution(9738500325315132338)
XLA Ops:
  0.6 180.8 %shard_map.76 = (bf16[8,768,128]{2,1,0:T(8,128)(2,1)}, bf16[128,6144]{1,0:T(8,128)(2,1)}, f32[8,1,768]{2,1,0:T(1,128)}) custom-call(f32[1,6144]{1,0:T(1,128)} %gains.1, bf16[4,32,6144]{2,1,0:T(8,128)(2,1)} %inputs.1, bf16[4,32,6144]{2,1,0:T(8,128)(2,1)} %cotangent.1, bf16[6144,128]{1,0:T(8,128)(2,1)} %bitcast.12, bf16[128,6144]{1,0:T(8,128)(2,1)} %bitcast.13), custom_call_target="tpu_custom_call" | custom-call | flops 16106127360 | bytes 12582912 | tf_op jit(solution)/shard_map/pallas_call | solution.py:298
  181.5 0.0 copy-start
  181.5 3.4 %bitcast_convert_fusion.1 = f32[1,6144,128]{2,1,0:T(8,128)} fusion(bf16[1,6144,128]{2,1,0:T(8,128)(2,1)} %bitcast.10), kind=kLoop, calls=%fused_computation.1 | loop fusion | flops 786432 | bytes 4718592 | tf_op jit(solution)/shard_map/convert_element_type | solution.py:341
  184.9 0.0 copy-done
  184.9 0.0 copy-start.1
  184.9 2.0 %bitcast_convert_fusion = f32[1,128,6144]{2,1,0:T(8,128)} fusion(bf16[128,6144]{1,0:T(8,128)(2,1)S(1)} %copy-done), kind=kLoop, calls=%fused_computation | loop fusion | flops 786432 | bytes 4718592 | tf_op jit(solution)/shard_map/convert_element_type | solution.py:342
  186.9 0.0 copy-done.1
  186.9 0.6 copy.9
Async XLA Ops:
  181.5 3.4 %copy-start = (bf16[128,6144]{1,0:T(8,128)(2,1)S(1)}, bf16[128,6144]{1,0:T(8,128)(2,1)}, u32[]{:S(2)}) copy-start(bf16[128,6144]{1,0:T(8,128)(2,1)} %get-tuple-element.7) | copy-start | bytes 4718596
  184.9 2.0 %copy-start.1 = (f32[8,1,768]{2,1,0:T(1,128)S(1)}, f32[8,1,768]{2,1,0:T(1,128)}, u32[]{:S(2)}) copy-start(f32[8,1,768]{2,1,0:T(1,128)} %get-tuple-element.8) | copy-start | bytes 73732

commit v4 on v3

--- a/solution.py
+++ b/solution.py
@@ -259,13 +259,26 @@
         return carry
 
     lax.fori_loop(0, layers, backward, 0)
+    def early(k):
+        return ((k == n_pipe // 2) | (k == n_pipe // 4) | (k == 0)) & (lax.rem(me + k, n_pipe) != 0)
+
+    def send_early(k, carry):
+        @pl.when(early(k))
+        def _():
+            send_out(lax.rem(me + k, n_pipe))
+
+        return carry
+
+    def send_late(k, carry):
+        @pl.when(jnp.logical_not(early(k)))
+        def _():
+            send_out(lax.rem(me + k, n_pipe))
+
+        return carry
+
+    lax.fori_loop(0, n_pipe, send_early, 0)
     gradients(0)
-
-    def send_all(k, carry):
-        send_out(lax.rem(me + k, n_pipe))
-        return carry
-
-    lax.fori_loop(0, n_pipe, send_all, 0)
+    lax.fori_loop(0, n_pipe, send_late, 0)
 
     for k in range(1, n_pipe):
         for copy in weight_copies(k):

time: 189 us -> 184 us (0.974)
  Pallas kernels: 181 us -> 176 us
    pallas_call x1, Pallas kernels: 181 us -> 176 us  [per_device(): pl.pallas_call(functools.partial(kernel, n_pipe, n_dp), out_shape=(jax.Sh...]
where the time goes in v4:
time: 184 us; the launch traced here: 182 us
  Pallas kernels  176 us (96%)
  other arithmetic  5.37 us (3%)
    pallas_call x1, Pallas kernels, per_device(): pl.pallas_call(functools.partial(kernel, n_pipe, n_dp), out_shape=(jax.Sh...  176 us

profile of v4, /device:TPU:0, one launch (start us, length us, event | category | flops | bytes accessed | tf_op | source)
XLA Modules:
  0.0 182.5 jit_solution(18030425023243543734)
XLA Ops:
  0.6 175.8 %shard_map.76 = (bf16[8,768,128]{2,1,0:T(8,128)(2,1)}, bf16[128,6144]{1,0:T(8,128)(2,1)}, f32[8,1,768]{2,1,0:T(1,128)}) custom-call(f32[1,6144]{1,0:T(1,128)} %gains.1, bf16[4,32,6144]{2,1,0:T(8,128)(2,1)} %inputs.1, bf16[4,32,6144]{2,1,0:T(8,128)(2,1)} %cotangent.1, bf16[6144,128]{1,0:T(8,128)(2,1)} %bitcast.12, bf16[128,6144]{1,0:T(8,128)(2,1)} %bitcast.13), custom_call_target="tpu_custom_call" | custom-call | flops 16106127360 | bytes 12582912 | tf_op jit(solution)/shard_map/pallas_call | solution.py:311
  176.5 0.0 copy-start
  176.5 3.4 %bitcast_convert_fusion.1 = f32[1,6144,128]{2,1,0:T(8,128)} fusion(bf16[1,6144,128]{2,1,0:T(8,128)(2,1)} %bitcast.10), kind=kLoop, calls=%fused_computation.1 | loop fusion | flops 786432 | bytes 4718592 | tf_op jit(solution)/shard_map/convert_element_type | solution.py:354
  179.9 0.0 copy-done
  179.9 0.0 copy-start.1
  179.9 2.0 %bitcast_convert_fusion = f32[1,128,6144]{2,1,0:T(8,128)} fusion(bf16[128,6144]{1,0:T(8,128)(2,1)S(1)} %copy-done), kind=kLoop, calls=%fused_computation | loop fusion | flops 786432 | bytes 4718592 | tf_op jit(solution)/shard_map/convert_element_type | solution.py:355
  181.8 0.0 copy-done.1
  181.8 0.6 copy.9
Async XLA Ops:
  176.5 3.4 %copy-start = (bf16[128,6144]{1,0:T(8,128)(2,1)S(1)}, bf16[128,6144]{1,0:T(8,128)(2,1)}, u32[]{:S(2)}) copy-start(bf16[128,6144]{1,0:T(8,128)(2,1)} %get-tuple-element.7) | copy-start | bytes 4718596
  179.9 2.0 %copy-start.1 = (f32[8,1,768]{2,1,0:T(1,128)S(1)}, f32[8,1,768]{2,1,0:T(1,128)}, u32[]{:S(2)}) copy-start(f32[8,1,768]{2,1,0:T(1,128)} %get-tuple-element.8) | copy-start | bytes 73732
